TPU v7x, 512 devices: a whole 4x4x16 slice. The times are simulated.
512 devices in a mesh: pool: 128 (over z, y, core), tp: 4 (over x).
Axes of the slice: x: 4, y: 4, z: 16, core: 2. Of those that a mesh axis runs over, the one named last changes fastest.
Arguments:
- queries: bfloat16 [16384, 64, 128], P(('pool', 'tp')), may hold values from -6 to 6
- fresh_key_values: bfloat16 [16384, 4, 2, 128], P(('pool', 'tp')), may hold values from -5 to 5
- pooled_page_cache: bfloat16 [5, 128, 8, 4, 2, 128], P(None, 'pool', None, 'tp'), may hold values from -5 to 5
- leaf_cache: bfloat16 [128, 256, 4, 2, 128], P('pool', None, 'tp'), may hold values from -5 to 5
- parent: int32 [133], replicated, may hold values from 0 to 4, as said below
- node_pages: int32 [5], replicated, may hold values from 64 to 128
- node_owner: int32 [5], replicated, may hold values from 0 to 127
- leaf_len: int32 [128], P('pool'), may hold values from 1 to 32
Outputs:
- attended: bfloat16 [16384, 64, 128], P(('pool', 'tp'))
Inputs may be any that keep to these rules, and one draw needn't show every extreme that they name: Nodes 0 to 4 have parent 0; node 5 + r is request r's own node and its parent is one of nodes 1 to 4.
All inputs are finite; a program needn't handle non-finite values.
Results may differ from a plain program's by a relative error of at most 0.008.
Values may be sent and summed in bfloat16 or wider, within the bound.
A program may use at most 64 MiB of HBM per device.

v0:
```python
import jax
import jax.numpy as jnp
from jax import lax
from jax.sharding import PartitionSpec as P


def attend(carried, query_tile, key_pairs, key_mask, batched):
    running, totals, accum = carried
    inv_root = query_tile.shape[-1] ** (-0.5)
    score_form = "btkgd,bskd->btkgs" if batched else "btkgd,skd->btkgs"
    value_form = "btkgs,bskd->btkgd" if batched else "btkgs,skd->btkgd"
    scores = (
        jnp.einsum(score_form, query_tile, key_pairs[..., 0, :], preferred_element_type=jnp.float32)
        * inv_root
    )
    wide_mask = key_mask[:, :, None, None, :]
    scores = jnp.where(wide_mask, scores, jnp.float32(-1e30))
    new_max = jnp.maximum(running, jnp.max(scores, axis=-1))
    weights = jnp.where(wide_mask, jnp.exp(scores - new_max[..., None]), jnp.float32(0.0))
    rescale = jnp.exp(running - new_max)
    totals = totals * rescale + jnp.sum(weights, axis=-1)
    accum = accum * rescale[..., None] + jnp.einsum(
        value_form,
        weights.astype(jnp.bfloat16),
        key_pairs[..., 1, :],
        preferred_element_type=jnp.float32,
    )
    return (new_max, totals, accum)


def per_device(
    queries,
    fresh_key_values,
    pooled_page_cache,
    leaf_cache,
    parent,
    node_pages,
    node_owner,
    leaf_len,
):
    heads_q, heads_kv = (
        lax.all_to_all(queries, "tp", split_axis=1, concat_axis=0, tiled=True),
        lax.all_to_all(fresh_key_values, "tp", split_axis=1, concat_axis=0, tiled=True),
    )
    pool_size = lax.axis_size("pool")
    pool_index = lax.axis_index("pool")
    requests = leaf_cache.shape[0]
    tile_rows = heads_q.shape[0] // requests
    kv_local = heads_kv.shape[1]
    query_group_width = heads_q.shape[1] // kv_local
    head_dim = heads_q.shape[2]
    page_len = pooled_page_cache.shape[2]
    shared_count = pooled_page_cache.shape[0]
    mids_count = shared_count - 1
    query_tile = heads_q.reshape(requests, tile_rows, kv_local, query_group_width, head_dim)
    suffix_kv = heads_kv.reshape(requests, tile_rows, kv_local, 2, head_dim)
    my_mids = lax.dynamic_slice_in_dim(parent, 1 + mids_count + pool_index * requests, requests)
    carried = (
        jnp.full((requests, tile_rows, kv_local, query_group_width), -1e30, jnp.float32),
        jnp.zeros((requests, tile_rows, kv_local, query_group_width), jnp.float32),
        jnp.zeros((requests, tile_rows, kv_local, query_group_width, head_dim), jnp.float32),
    )
    fold_carried = carried
    pieces = lax.all_gather(pooled_page_cache, "pool", axis=1, tiled=True)
    stripes = pieces.shape[1]
    slot_ids = jnp.arange(stripes, dtype=jnp.int32)
    for node_id in range(shared_count):
        usable = jnp.mod(slot_ids - node_owner[node_id], pool_size) < node_pages[node_id]
        usable = jnp.repeat(usable, page_len)
        if node_id == 0:
            relevant = jnp.ones((requests,), bool)
        else:
            relevant = my_mids == node_id
        key_mask = relevant[:, None, None] & usable[None, None, :]
        key_pairs = pieces[node_id].reshape(stripes * page_len, kv_local, 2, head_dim)
        fold_carried = attend(fold_carried, query_tile, key_pairs, key_mask, False)
    carried = fold_carried
    leaf_mask = (
        jnp.arange(leaf_cache.shape[1], dtype=jnp.int32)[None, :] < (leaf_len * page_len)[:, None]
    )
    carried = attend(carried, query_tile, leaf_cache, leaf_mask[:, None, :], True)
    row_ids = jnp.arange(tile_rows, dtype=jnp.int32)
    causal = (row_ids[None, :] <= row_ids[:, None])[None]
    carried = attend(carried, query_tile, suffix_kv, causal, True)
    running, totals, accum = carried
    result = (accum / totals[..., None]).astype(jnp.bfloat16)
    result = result.reshape(requests * tile_rows, kv_local * query_group_width, head_dim)
    return lax.all_to_all(result, "tp", split_axis=0, concat_axis=1, tiled=True)


def solution(mesh):
    return jax.shard_map(
        per_device,
        mesh=mesh,
        in_specs=(
            P(("pool", "tp"), None, None),
            P(("pool", "tp"), None, None, None),
            P(None, "pool", None, "tp", None, None),
            P("pool", None, "tp", None, None),
            P(),
            P(),
            P(),
            P("pool"),
        ),
        out_specs=P(("pool", "tp"), None, None),
        check_vma=False,
    )
```

profile of v0, /device:TPU:1, one launch (start us, length us, event | category | flops | bytes accessed | tf_op | source)
XLA Modules:
  0.0 224.5 jit_solution(6503570099728563869)
XLA Ops:
  7.3 1.5 copy.58
  8.8 4.8 %all-to-all-start.1 = ((bf16[32,4,2,128]{3,2,0,1:T(2,128)(2,1)}), bf16[32,4,2,128]{3,2,0,1:T(2,128)(2,1)S(1)}, u32[]{:S(2)}, u32[]{:S(2)}) async-start(bf16[32,4,2,128]{3,2,0,1:T(2,128)(2,1)} %copy.58), calls=%async_computation.1 | async-start | bytes 131072 | tf_op jit(solution)/shard_map/all_to_all | solution.py:43
  14.2 1.3 dynamic_slice.3
  17.7 1.5 fusion.161
  19.2 1.5 fusion.160
  20.7 1.3 fusion.130
  22.0 1.3 compare_and_fusion
  24.4 1.3 compare_and_fusion.2
  25.7 2.2 copy.44
  28.6 4.2 %all-to-all-start = ((bf16[32,64,128]{2,0,1:T(8,128)(2,1)}), bf16[32,64,128]{2,0,1:T(8,128)(2,1)S(1)}, u32[]{:S(2)}, u32[]{:S(2)}) async-start(bf16[32,64,128]{2,0,1:T(8,128)(2,1)} %copy.44), calls=%async_computation | async-start | bytes 1048576 | tf_op jit(solution)/shard_map/all_to_all | solution.py:42
  32.8 1.4 compare_and_fusion.3
  36.4 3.3 %all-to-all-done = bf16[32,64,128]{2,0,1:T(8,128)(2,1)S(1)} async-done(((bf16[32,64,128]{2,0,1:T(8,128)(2,1)}), bf16[32,64,128]{2,0,1:T(8,128)(2,1)S(1)}, u32[]{:S(2)}, u32[]{:S(2)}) %all-to-all-start) | async-done | bytes 524320 | tf_op jit(solution)/shard_map/all_to_all | solution.py:42
  39.8 1.3 fusion.162
  41.6 109.0 %all-gather.2.cloned.1.call-done = bf16[5,128,8,1,2,128]{5,4,3,2,1,0:T(2,128)(2,1)} async-done(((bf16[5,1,8,1,2,128]{5,4,3,2,1,0:T(2,128)(2,1)}), bf16[5,128,8,1,2,128]{5,4,3,2,1,0:T(2,128)(2,1)}) %all-gather.2.cloned.1.call-update) | async-done | bytes 2621456 | tf_op jit(solution)/shard_map/all_gather | solution.py:64
  150.6 3.1 %fusion.158 = (bf16[1,128,8,1,2,128]{5,4,3,2,1,0:T(2,128)(2,1)S(1)}, bf16[1,128,8,1,2,128]{5,4,3,2,1,0:T(2,128)(2,1)S(1)}, bf16[1,128,8,1,2,128]{5,4,3,2,1,0:T(2...) fusion(bf16[5,128,8,1,2,128]{5,4,3,2,1,0:T(2,128)(2,1)} %all-gather.2.cloned.1.call-done), kind=kLoop, calls=%fused_computation.185 | loop fusion | bytes 5242880 | tf_op jit(solution)/shard_map/slice | solution.py:75
  153.8 1.3 bitcast_reduce_fusion
  155.3 1.3 bitcast_reduce_fusion.1
  156.7 1.3 bitcast_reduce_fusion.2
  158.2 4.1 %bitcast_reduce_fusion.3 = (f32[128,16]{0,1:T(8,128)S(1)}, f32[1024,128,16]{1,0,2:T(8,128)}) fusion(pred[1024]{0:T(1024)(128)(4,1)S(1)} %and.107, bf16[128,16,128]{2,0,1:T(8,128)(2,1)S(1)} %bitcast.505, bf16[1024,1,2,128]{3,0,2,1:T(8,128)(2,1)S(1)} %get-tuple-element.53), kind=kOutput, calls=%fused_computation.16 | convolution fusion | flops 543160320 | bytes 9184256 | tf_op jit(solution)/shard_map/btkgd,skd->btkgs/dot_general | solution.py:13
  162.2 4.1 %bitcast_reduce_fusion.4 = (f32[128,16]{0,1:T(8,128)S(1)}, f32[1024,128,16]{1,0,2:T(8,128)}) fusion(pred[1024]{0:T(1024)(128)(4,1)S(1)} %broadcast_in_dim.161, bf16[128,16,128]{2,0,1:T(8,128)(2,1)S(1)} %bitcast.506, bf16[1024,1,2,128]{3,0,2,1:T(8,128)(2,1)S(1)} %get-tuple-element.54), kind=kOutput, calls=%fused_computation.21 | convolution fusion | flops 543160320 | bytes 9184256 | tf_op jit(solution)/shard_map/btkgd,skd->btkgs/dot_general | solution.py:13
  166.9 2.0 convolution_bitcast_fusion.1
  169.1 2.6 %fusion.18 = f32[128,16]{0,1:T(8,128)S(1)} fusion(f32[1024,128,16]{1,0,2:T(8,128)S(1)} %get-tuple-element.42, f32[128,16]{0,1:T(8,128)S(1)} %get-tuple-element.14, pred[1024]{0:T(1024)(128)(4,1)S(1)} %and.122), kind=kLoop, calls=%fused_computation.33 | loop fusion | flops 10483712 | bytes 8406016 | tf_op jit(solution)/shard_map/reduce_sum | solution.py:21
  171.7 2.8 %fusion.16 = f32[128,16]{0,1:T(8,128)S(1)} fusion(f32[1024,128,16]{1,0,2:T(8,128)S(1)} %get-tuple-element.44, f32[128,16]{0,1:T(8,128)S(1)} %get-tuple-element.15, pred[1024]{0:T(1024)(128)(4,1)S(1)} %and.117), kind=kLoop, calls=%fused_computation.31 | loop fusion | flops 10483712 | bytes 8406016 | tf_op jit(solution)/shard_map/reduce_sum | solution.py:21
  174.5 2.6 %fusion.14 = f32[128,16]{0,1:T(8,128)S(1)} fusion(f32[1024,128,16]{1,0,2:T(8,128)S(1)} %get-tuple-element.46, f32[128,16]{0,1:T(8,128)S(1)} %get-tuple-element.16, pred[1024]{0:T(1024)(128)(4,1)S(1)} %and.112), kind=kLoop, calls=%fused_computation.29 | loop fusion | flops 10483712 | bytes 8406016 | tf_op jit(solution)/shard_map/reduce_sum | solution.py:21
  177.1 2.6 %fusion.12 = f32[128,16]{0,1:T(8,128)S(1)} fusion(f32[1024,128,16]{1,0,2:T(8,128)S(1)} %bitcast.508, f32[128,16]{0,1:T(8,128)S(1)} %get-tuple-element.17, pred[1024]{0:T(1024)(128)(4,1)S(1)} %and.107), kind=kLoop, calls=%fused_computation.27 | loop fusion | flops 10483712 | bytes 8406016 | tf_op jit(solution)/shard_map/reduce_sum | solution.py:21
  179.7 4.6 %fusion.10 = f32[128,16]{0,1:T(8,128)S(1)} fusion(f32[1024,128,16]{1,0,2:T(8,128)} %get-tuple-element.50, f32[128,16]{0,1:T(8,128)S(1)} %get-tuple-element.26, pred[1024]{0:T(1024)(128)(4,1)S(1)} %broadcast_in_dim.161), kind=kLoop, calls=%fused_computation.25 | loop fusion | flops 10483712 | bytes 8406016 | tf_op jit(solution)/shard_map/reduce_sum | solution.py:21
  184.4 6.4 %fusion.97 = f32[1,128,1,128,16]{1,3,4,2,0:T(8,128)S(1)} fusion(f32[1024,128,16]{1,0,2:T(8,128)} %get-tuple-element.50, f32[128,16]{0,1:T(8,128)S(1)} %get-tuple-element.26, pred[1024]{0:T(1024)(128)(4,1)S(1)} %broadcast_in_dim.161, f32[128,16]{0,1:T(8,128)S(1)} %get-tuple-element.11, f32[128,16]{0,1:T(8,128)S(1)} %get-tuple-element.25, ...), kind=kOutput, calls=%fused_computation.83 | convolution fusion | flops 547880960 | bytes 9725952 | tf_op jit(solution)/shard_map/btkgs,skd->btkgd/dot_general | solution.py:22
  190.7 3.1 %fusion.94 = f32[1,128,1,128,16]{1,3,4,2,0:T(8,128)S(1)} fusion(f32[1,128,1,128,16]{1,3,4,2,0:T(8,128)S(1)} %fusion.97, f32[1024,128,16]{1,0,2:T(8,128)S(1)} %bitcast.508, f32[128,16]{0,1:T(8,128)S(1)} %get-tuple-element.17, pred[1024]{0:T(1024)(128)(4,1)S(1)} %and.107, f32[128,16]{0,1:T(8,128)S(1)} %get-tuple-element.10, ...), kind=kOutput, calls=%fused_computation.82 | convolution fusion | flops 547880960 | bytes 10766336 | tf_op jit(solution)/shard_map/btkgs,skd->btkgd/dot_general | solution.py:22
  193.8 3.1 %fusion.91 = f32[1,128,1,128,16]{1,3,4,2,0:T(8,128)S(1)} fusion(f32[1,128,1,128,16]{1,3,4,2,0:T(8,128)S(1)} %fusion.94, f32[1024,128,16]{1,0,2:T(8,128)S(1)} %get-tuple-element.46, f32[128,16]{0,1:T(8,128)S(1)} %get-tuple-element.16, pred[1024]{0:T(1024)(128)(4,1)S(1)} %and.112, f32[128,16]{0,1:T(8,128)S(1)} %get-tuple-element.9, ...), kind=kOutput, calls=%fused_computation.81 | convolution fusion | flops 547880960 | bytes 10766336 | tf_op jit(solution)/shard_map/btkgs,skd->btkgd/dot_general | solution.py:22
  196.9 3.1 %fusion.88 = f32[1,128,1,128,16]{1,3,4,2,0:T(8,128)S(1)} fusion(f32[1,128,1,128,16]{1,3,4,2,0:T(8,128)S(1)} %fusion.91, f32[1024,128,16]{1,0,2:T(8,128)S(1)} %get-tuple-element.44, f32[128,16]{0,1:T(8,128)S(1)} %get-tuple-element.15, pred[1024]{0:T(1024)(128)(4,1)S(1)} %and.117, f32[128,16]{0,1:T(8,128)S(1)} %get-tuple-element.8, ...), kind=kOutput, calls=%fused_computation.80 | convolution fusion | flops 547880960 | bytes 10766336 | tf_op jit(solution)/shard_map/btkgs,skd->btkgd/dot_general | solution.py:22
  200.0 3.1 %fusion.103 = f32[1,128,1,16,128]{4,1,3,0,2:T(8,128)S(1)} fusion(f32[1,128,1,16,128]{4,1,3,0,2:T(8,128)S(1)} %copy-done.2, f32[1,128,1,128,16]{1,3,4,2,0:T(8,128)S(1)} %fusion.88, f32[1024,128,16]{1,0,2:T(8,128)S(1)} %get-tuple-element.42, f32[128,16]{0,1:T(8,128)S(1)} %get-tuple-element.14, pred[1024]{0:T(1024)(128)(4,1)S(1)} %and.122, ...), kind=kOutput, calls=%fused_computation.85 | convolution fusion | flops 548405248 | bytes 11823104 | tf_op jit(solution)/shard_map/btkgs,skd->btkgd/dot_general | solution.py:22
  204.0 12.8 %all_to_all.48 = bf16[128,16,128]{2,1,0:T(8,128)(2,1)S(1)} all-to-all(bf16[128,16,128]{2,1,0:T(8,128)(2,1)S(1)} %copy.61), channel_id=1, replica_groups=mesh['pool'=128,'tp'=4] {'tp'}, dimensions={0} | all-to-all | bytes 1048576 | tf_op jit(solution)/shard_map/all_to_all | solution.py:88
  (41 shorter events, 7.5 us)
Async XLA Ops:
  6.5 144.1 %all-gather.2.cloned.1.call-start = ((), (), s32[]{:S(2)}) async-start(), calls=%async_computation.3 | async-start | bytes 2641920 | tf_op jit(solution)/shard_map/all_gather | solution.py:64
  8.8 19.8 %all-to-all-start.1 = ((bf16[32,4,2,128]{3,2,0,1:T(2,128)(2,1)}), bf16[32,4,2,128]{3,2,0,1:T(2,128)(2,1)S(1)}, u32[]{:S(2)}, u32[]{:S(2)}) async-start(bf16[32,4,2,128]{3,2,0,1:T(2,128)(2,1)} %copy.58), calls=%async_computation.1 | async-start | bytes 131072 | tf_op jit(solution)/shard_map/all_to_all | solution.py:43
  28.6 11.2 %all-to-all-start = ((bf16[32,64,128]{2,0,1:T(8,128)(2,1)}), bf16[32,64,128]{2,0,1:T(8,128)(2,1)S(1)}, u32[]{:S(2)}, u32[]{:S(2)}) async-start(bf16[32,64,128]{2,0,1:T(8,128)(2,1)} %copy.44), calls=%async_computation | async-start | bytes 1048576 | tf_op jit(solution)/shard_map/all_to_all | solution.py:42
  162.2 6.7 %copy-start = (f32[1,128,1,16,128]{1,4,3,2,0:T(8,128)S(1)}, f32[1,128,1,16,128]{1,4,3,2,0:T(8,128)}, u32[]{:S(2)}) copy-start(f32[1,128,1,16,128]{1,4,3,2,0:T(8,128)} %get-tuple-element.38) | copy-start | bytes 3145732
  171.7 5.4 %slice-start = ((s8[8388608]{0:T(1024)(128)(4,1)}), s8[4194304]{0:T(1024)(128)(4,1)S(1)}, s32[]{:S(2)}) async-start(s8[8388608]{0:T(1024)(128)(4,1)} %bitcast.507), calls=%async_computation.4 | async-start | bytes 8388608
  174.5 2.6 %slice-start.1 = ((s8[8388608]{0:T(1024)(128)(4,1)}), s8[4194304]{0:T(1024)(128)(4,1)S(1)}, s32[]{:S(2)}) async-start(s8[8388608]{0:T(1024)(128)(4,1)} %bitcast.507), calls=%async_computation.5 | async-start | bytes 8388608
  196.9 3.1 %copy-start.2 = (f32[1,128,1,16,128]{4,1,3,0,2:T(8,128)S(1)}, f32[1,128,1,16,128]{4,1,3,0,2:T(8,128)}, u32[]{:S(2)}) copy-start(f32[1,128,1,16,128]{4,1,3,0,2:T(8,128)} %convolution_bitcast_fusion.1) | copy-start | bytes 3145732
  199.9 3.2 %copy-start.1 = (f32[1,128,1,16,128]{1,4,3,2,0:T(8,128)S(1)}, f32[1,128,1,16,128]{1,4,3,2,0:T(8,128)}, u32[]{:S(2)}) copy-start(f32[1,128,1,16,128]{1,4,3,2,0:T(8,128)} %get-tuple-element.38) | copy-start | bytes 3145732
Sparse Core Ops, SparseCore 0:
  10.4 140.2 all-gather.1
where the time goes:
time: 225 us; the launch traced here: 224 us
  waiting for transfers between devices  113 us (50%)
  matrix products  35.1 us (16%)
  other arithmetic  22.4 us (10%)
  between operations  17.2 us (8%)
  local copies, waits for them, and re-layouts  14.9 us (7%)
  blocking collectives  12.8 us (6%)
  starting transfers between devices  9.09 us (4%)
    all_gather x1, waiting for transfers between devices, per_device(): pieces = lax.all_gather(pooled_page_cache, 'pool', axis=1, tiled=True)  109 us
    dot_general x7, matrix products, attend(): jnp.einsum(value_form, weights.astype(jnp.bfloat16), key_pairs[..., 1, :]...  21.2 us
    reduce_sum x7, other arithmetic, attend(): totals = totals * rescale + jnp.sum(weights, axis=-1)  16 us
    dot_general x7, matrix products, attend(): jnp.einsum(score_form, query_tile, key_pairs[..., 0, :], preferred_elemen...  13.9 us
    all_to_all x1, blocking collectives, per_device(): return lax.all_to_all(result, 'tp', split_axis=0, concat_axis=1, tiled=True)  12.8 us
    and x4, other arithmetic, per_device(): key_mask = relevant[:, None, None] & usable[None, None, :]  5.03 us
    all_to_all x1, starting transfers between devices, per_device(): lax.all_to_all(fresh_key_values, 'tp', split_axis=1, concat_axis=0, tiled...  4.84 us
  transfers between devices with their start and end apart: 3, of which 2 were waited for; matrix products, arithmetic and copies ran while one was open for 8% of the time, Pallas kernels for 0%

commit v1 on v0

v1 whole, which is shorter than its diff:
```python
import jax
import jax.numpy as jnp
from jax import lax
from jax.experimental import pallas as pl
from jax.experimental.pallas import tpu as pltpu
from jax.sharding import PartitionSpec as P

MESH = pl.DeviceIdType.MESH
BF, F32, I32 = jnp.bfloat16, jnp.float32, jnp.int32
NEG = -1e30

REL = (0, 1, -1, 2, -2, 5, -5, 4, 6, 3, 7, -4, -6, -3, -7, 8)
EARLY, LATE = (0, 7), (7, 16)
GROUPS = ((0, 1), (1, 5), (5, 7), (7, 16))


def dot_t(a, b):
    return lax.dot_general(a, b, (((1,), (1,)), ((), ())), preferred_element_type=F32)


def kernel(
    parent, pages, owners, leaf_len, queries, fresh, pooled, leaf, out,
    q_all, k1, v1, k2, v2, k3, v3, b1, b2, b3, wide, fresh_out,
    z_own, z_near, z_far, z_rest, to_y, held, other, m_ref, acc, o_all,
    zs, zr, ys, yr, cs, cr, qs, qr, fs, fr, os, orr, local,
):
    pool, x = lax.axis_index("pool"), lax.axis_index("tp")
    z, y, c = pool // 8, (pool // 2) % 4, pool % 2

    def at(dz=0, dy=0, dc=0, dx=0):
        place = ((z + dz + 16) % 16) * 8 + ((y + dy) % 4) * 2 + (c + dc) % 2
        return (place, (x + dx) % 4)

    peers = [at(dx=1), at(dx=2), at(dx=3), at(dy=1), at(dy=2), at(dy=3), at(dc=1)]
    peers += [at(dz=d) for d in (1, -1, 2, -2, 3, -3, 5, -5)]
    barrier = pltpu.get_barrier_semaphore()
    for peer in peers:
        pl.semaphore_signal(barrier, inc=1, device_id=peer, device_id_type=MESH)

    own_q = pltpu.make_async_copy(
        queries.at[:, pl.ds(pl.multiple_of(x * 16, 16), 16)],
        q_all.at[pl.ds(pl.multiple_of(x * 32, 32), 32)],
        local.at[0],
    )
    own_q.start()

    wide[0:80] = pooled[...].astype(F32)
    for n in range(5):
        keys = wide[pl.ds(16 * n, 8, stride=2)]
        values = wide[pl.ds(16 * n + 1, 8, stride=2)]
        z_own[0, n] = jnp.concatenate([keys, values], 0).astype(BF)
    wide[128:384] = fresh[...].astype(F32)
    for h in range(4):
        for kv in range(2):
            fresh_out[h, kv] = wide[pl.ds(128 + 2 * h + kv, 32, stride=8)].astype(BF)

    pl.semaphore_wait(barrier, len(peers))

    def send(src, dst, s, r, peer):
        copy = pltpu.make_async_remote_copy(
            src_ref=src, dst_ref=dst, send_sem=s, recv_sem=r, device_id=peer, device_id_type=MESH
        )
        copy.start()
        return copy

    started = []

    def send_z(k, src, dst, dz):
        copy = send(src, dst, zs.at[k], zr.at[k], at(dz=dz))
        started.append(copy)
        return copy

    far = [send_z(0, z_own.at[0], z_far.at[1], 5), send_z(1, z_own.at[0], z_far.at[0], -5)]
    near = [
        send_z(2 + i, z_own.at[0], z_near.at[i], d) for i, d in enumerate((-1, 1, -2, 2))
    ]

    mid = [
        [parent[5 + at(dy=j)[0] - c + cc] for cc in range(2)] for j in range(4)
    ]

    def send_y(g, zone):
        lo, hi = GROUPS[g]
        slots = pl.ds(lo, hi - lo)
        for j in (2, 1, 3):
            to_y[j - 1, 0, slots] = zone[:, 0]
            for cc in range(2):
                to_y[j - 1, 1 + cc, slots] = zone[:, mid[j][cc]]
        copies = []
        for j in (2, 1, 3):
            copies.append(
                send(
                    to_y.at[j - 1, :, slots],
                    held.at[:, 4 - j, slots],
                    ys.at[g, j - 1],
                    yr.at[g, j - 1],
                    at(dy=j),
                )
            )
        held[0, 0, slots] = zone[:, 0]
        for cc in range(2):
            held[1 + cc, 0, slots] = zone[:, mid[0][cc]]
        started.extend(copies)
        return copies

    early_y = send_y(0, z_own)

    q_in = []
    for j in (2, 1, 3):
        head = pl.multiple_of(((x + j) % 4) * 16, 16)
        q_in.append(
            send(
                queries.at[:, pl.ds(head, 16)],
                q_all.at[pl.ds(pl.multiple_of(x * 32, 32), 32)],
                qs.at[j - 1],
                qr.at[j - 1],
                at(dx=j),
            )
        )
    rows_x = pl.ds(pl.multiple_of(x * 32, 32), 32)
    f_in = []
    for j in (2, 1, 3):
        for kv in range(2):
            f_in.append(
                send(
                    fresh_out.at[(x + j) % 4, kv],
                    (k1 if kv == 0 else v1).at[rows_x, pl.ds(0, 128)],
                    fs.at[j - 1, kv],
                    fr.at[j - 1, kv],
                    at(dx=j),
                )
            )
    k1[rows_x, :] = fresh_out[x, 0]
    v1[rows_x, 0:128] = fresh_out[x, 1]

    for part in range(2):
        wide[0:256] = leaf[pl.ds(part * 256, 256)].astype(F32)
        k1[128 + part * 128 : 256 + part * 128] = wide[pl.ds(0, 128, stride=2)].astype(BF)
        v1[128 + part * 128 : 256 + part * 128, 0:128] = wide[pl.ds(1, 128, stride=2)].astype(BF)
    v1[:, 128:256] = jnp.ones((384, 128), BF)
    v2[:, 128:256] = jnp.ones((896, 128), BF)
    v3[:, 128:256] = jnp.ones((1152, 128), BF)

    b1[...] = jnp.where(lax.broadcasted_iota(I32, (8, 256), 1) < leaf_len[0] * 8, 0.0, NEG)

    my_mid = parent[5 + pool]

    def used_bias(ref, lo, hi):
        count = hi - lo
        block = 4 * count * 8
        col = lax.broadcasted_iota(I32, (8, 4 * block), 1)
        part = sum((col >= block * k).astype(I32) for k in range(1, 4))
        rest = col - part * block
        dy = sum((rest >= count * 8 * k).astype(I32) for k in range(1, 4))
        slot = (rest - dy * (count * 8)) // 8
        rel = jnp.zeros_like(slot)
        for k in range(count):
            rel = jnp.where(slot == k, (z + REL[lo + k] + 16) % 16, rel)
        core = jnp.where(part % 2 == 0, c, 1 - c)
        place = rel * 8 + ((y + dy) & 3) * 2 + core
        in_root = part < 2
        first = jnp.where(in_root, owners[0], owners[my_mid])
        many = jnp.where(in_root, pages[0], pages[my_mid])
        ref[...] = jnp.where(((place - first) & 127) < many, 0.0, NEG)

    used_bias(b2, *EARLY)
    used_bias(b3, *LATE)

    for copy in near:
        copy.wait_recv()
    early_y += send_y(1, z_near)
    for copy in far:
        copy.wait_recv()
    rest = []
    for f in range(2):
        for i, d in enumerate((1, -1, 2, -2)):
            if f == 0:
                slot = {1: 0, -1: 1, 2: 2, -2: 3}[d]
            else:
                slot = {-1: 4, 1: 5, -2: 6, 2: 7}[d]
            rest.append(send_z(6 + 4 * f + i, z_far.at[f], z_rest.at[slot], d))
    rest.append(send_z(14, z_far.at[c], z_rest.at[8], 6 * c - 3))
    early_y += send_y(2, z_far)
    for copy in rest:
        copy.wait_recv()
    late_y = send_y(3, z_rest)

    def swap(k, lo, hi):
        slots = pl.ds(lo, hi - lo)
        pair = [
            send(held.at[0, :, slots], other.at[0, :, slots], cs.at[k, 0], cr.at[k, 0], at(dc=1)),
            send(held.at[2 - c, :, slots], other.at[1, :, slots], cs.at[k, 1], cr.at[k, 1], at(dc=1)),
        ]
        started.extend(pair)
        return pair

    def gather_keys(k_ref, v_ref, lo, hi):
        count = hi - lo
        size = 4 * count * 8
        slots = pl.ds(lo, count)
        parts = (held.at[0, :, slots], other.at[0, :, slots], held.at[1 + c, :, slots], other.at[1, :, slots])
        for n, ref in enumerate(parts):
            blocks = ref[...].astype(F32).reshape(4 * count, 16, 128)
            k_ref[n * size : (n + 1) * size] = blocks[:, 0:8].reshape(size, 128).astype(BF)
            v_ref[n * size : (n + 1) * size, 0:128] = blocks[:, 8:16].reshape(size, 128).astype(BF)

    for copy in early_y:
        copy.wait_recv()
    early_c = swap(0, *EARLY)

    scale = (128 ** -0.5) * 1.4426950408889634

    def chunk_of(step):
        return (x + step) % 4

    own_q.wait()
    for copy in q_in + f_in:
        copy.wait_recv()

    def phase1(step, _):
        part = chunk_of(step)
        rows = pl.ds(pl.multiple_of(part * 512, 512), 512)
        q = q_all[pl.ds(pl.multiple_of(part * 32, 32), 32)].reshape(512, 128)
        s_new = dot_t(q, k1[0:128])
        row = part * 32 + lax.broadcasted_iota(I32, (512, 128), 0) // 16
        s_new = jnp.where(lax.broadcasted_iota(I32, (512, 128), 1) <= row, s_new, NEG)
        s_leaf = dot_t(q, k1[128:384]) + b1[0:1]
        m = jnp.maximum(jnp.max(s_new, 1, keepdims=True), jnp.max(s_leaf, 1, keepdims=True))
        p_new = jnp.exp2((s_new - m) * scale).astype(BF)
        p_leaf = jnp.exp2((s_leaf - m) * scale).astype(BF)
        acc[rows] = jnp.dot(p_new, v1[0:128], preferred_element_type=F32) + jnp.dot(
            p_leaf, v1[128:384], preferred_element_type=F32
        )
        m_ref[rows] = m
        return 0

    lax.fori_loop(0, 4, phase1, 0)

    def fold(part, k_ref, v_ref, b_ref):
        rows = pl.ds(pl.multiple_of(part * 512, 512), 512)
        q = q_all[pl.ds(pl.multiple_of(part * 32, 32), 32)].reshape(512, 128)
        s = dot_t(q, k_ref[...]) + b_ref[0:1]
        old = m_ref[rows]
        m = jnp.maximum(old, jnp.max(s, 1, keepdims=True))
        p = jnp.exp2((s - m) * scale).astype(BF)
        total = acc[rows] * jnp.exp2((old - m) * scale) + jnp.dot(
            p, v_ref[...], preferred_element_type=F32
        )
        return m, total

    for copy in early_c:
        copy.wait_recv()
    gather_keys(k2, v2, *EARLY)

    def phase2(step, _):
        part = chunk_of(step)
        rows = pl.ds(pl.multiple_of(part * 512, 512), 512)
        m, total = fold(part, k2, v2, b2)
        m_ref[rows] = m
        acc[rows] = total
        return 0

    lax.fori_loop(0, 4, phase2, 0)

    for copy in late_y:
        copy.wait_recv()
    late_c = swap(1, *LATE)
    for copy in late_c:
        copy.wait_recv()
    gather_keys(k3, v3, *LATE)

    heads = pl.ds(pl.multiple_of(x * 16, 16), 16)
    results = []
    for j in (2, 1, 3, 0):
        part = (x + j) % 4
        _, total = fold(part, k3, v3, b3)
        tile = (total[:, 0:128] / total[:, 128:256]).astype(BF)
        span = pl.ds(pl.multiple_of(part * 32, 32), 32)
        o_all[span] = tile.reshape(32, 16, 128)
        if j:
            results.append(
                send(o_all.at[span], out.at[:, heads], os.at[j - 1], orr.at[j - 1], at(dx=j))
            )
        else:
            mine = pltpu.make_async_copy(o_all.at[span], out.at[:, heads], local.at[1])
            mine.start()
    mine.wait()
    for copy in started + q_in + f_in:
        copy.wait_send()
    for copy in results:
        copy.wait()


def per_device(queries, fresh, pooled, leaf, parent, pages, owners, leaf_len):
    vmem = pl.BlockSpec(memory_space=pltpu.VMEM)
    smem = pl.BlockSpec(memory_space=pltpu.SMEM)
    dma = pltpu.SemaphoreType.DMA

    def zone(n):
        return pltpu.VMEM((n, 5, 16, 128), BF)

    return pl.pallas_call(
        kernel,
        out_shape=jax.ShapeDtypeStruct((32, 64, 128), BF),
        in_specs=[smem] * 4 + [pl.BlockSpec(memory_space=pl.ANY), vmem, vmem, vmem],
        out_specs=pl.BlockSpec(memory_space=pl.ANY),
        scratch_shapes=[
            pltpu.VMEM((128, 16, 128), BF),
            pltpu.VMEM((384, 128), BF),
            pltpu.VMEM((384, 256), BF),
            pltpu.VMEM((896, 128), BF),
            pltpu.VMEM((896, 256), BF),
            pltpu.VMEM((1152, 128), BF),
            pltpu.VMEM((1152, 256), BF),
            pltpu.VMEM((8, 256), F32),
            pltpu.VMEM((8, 896), F32),
            pltpu.VMEM((8, 1152), F32),
            pltpu.VMEM((384, 128), F32),
            pltpu.VMEM((4, 2, 32, 128), BF),
            zone(1),
            zone(4),
            zone(2),
            zone(9),
            pltpu.VMEM((3, 3, 16, 16, 128), BF),
            pltpu.VMEM((3, 4, 16, 16, 128), BF),
            pltpu.VMEM((2, 4, 16, 16, 128), BF),
            pltpu.VMEM((2048, 1), F32),
            pltpu.VMEM((2048, 256), F32),
            pltpu.VMEM((128, 16, 128), BF),
            dma((15,)),
            dma((15,)),
            dma((4, 3)),
            dma((4, 3)),
            dma((2, 2)),
            dma((2, 2)),
            dma((3,)),
            dma((3,)),
            dma((3, 2)),
            dma((3, 2)),
            dma((3,)),
            dma((3,)),
            dma((2,)),
        ],
        compiler_params=pltpu.CompilerParams(
            collective_id=0, has_side_effects=True, vmem_limit_bytes=56 << 20
        ),
    )(
        parent,
        pages,
        owners,
        leaf_len,
        queries,
        fresh.reshape(256, 128),
        pooled.reshape(80, 128),
        leaf.reshape(512, 128),
    )


def solution(mesh):
    return jax.shard_map(
        per_device,
        mesh=mesh,
        in_specs=(
            P(("pool", "tp"), None, None),
            P(("pool", "tp"), None, None, None),
            P(None, "pool", None, "tp", None, None),
            P("pool", None, "tp", None, None),
            P(),
            P(),
            P(),
            P("pool"),
        ),
        out_specs=P(("pool", "tp"), None, None),
        check_vma=False,
    )
```

time: 225 us -> 50.3 us (0.22)
  waiting for transfers between devices: 113 us -> 0 us
  Pallas kernels: 0 us -> 47.6 us
  matrix products: 35.1 us -> 0 us
  other arithmetic: 22.4 us -> 0 us
  between operations: 17.2 us -> 0.66 us
  local copies, waits for them, and re-layouts: 14.9 us -> 1.87 us
  blocking collectives: 12.8 us -> 0 us
  starting transfers between devices: 9.09 us -> 0 us
    all_gather x1 -> x0, waiting for transfers between devices: 109 us -> none  [per_device(): pieces = lax.all_gather(pooled_page_cache, 'pool', axis=1, tiled=True)]
    pallas_call x0 -> x1, Pallas kernels: none -> 47.6 us  [per_device(): pl.pallas_call(kernel, out_shape=jax.ShapeDtypeStruct((32, 64, 128), BF),...]
    dot_general x14 -> x0, matrix products: 35.1 us -> none  [the longest x7 21.2 us: attend(): jnp.einsum(value_form, weights.astype(jnp.bfloat16), key_pairs[..., 1, :]...]
    reduce_sum x7 -> x0, other arithmetic: 16 us -> none  [attend(): totals = totals * rescale + jnp.sum(weights, axis=-1)]
    all_to_all x1 -> x0, blocking collectives: 12.8 us -> none  [per_device(): return lax.all_to_all(result, 'tp', split_axis=0, concat_axis=1, tiled=True)]
    all_to_all x2 -> x0, starting transfers between devices: 9.09 us -> none  [the longest x1 4.84 us: per_device(): lax.all_to_all(fresh_key_values, 'tp', split_axis=1, concat_axis=0, tiled...]
    slice x5 -> x0, local copies, waits for them, and re-layouts: 7.39 us -> none  [the longest x2 3.18 us: per_device(): pieces[node_id].reshape(stripes * page_len, kv_local, 2, head_dim)]
    and x4 -> x0, other arithmetic: 5.03 us -> none  [per_device(): key_mask = relevant[:, None, None] & usable[None, None, :]]
  transfers between devices with their start and end apart: 3 -> 0, of which waited for: 2 -> 0; matrix products, arithmetic and copies ran while one was open for 8% -> 0% of each run, Pallas kernels for 0% -> 0%
where the time goes in v1:
time: 50.3 us; the launch traced here: 50.2 us
  Pallas kernels  47.6 us (95%)
  local copies, waits for them, and re-layouts  1.87 us (4%)
  between operations  0.66 us (1%)
    pallas_call x1, Pallas kernels, per_device(): pl.pallas_call(kernel, out_shape=jax.ShapeDtypeStruct((32, 64, 128), BF),...  47.6 us
    unnamed x1, local copies, waits for them, and re-layouts  1.87 us

profile of v1, /device:TPU:1, one launch (start us, length us, event | category | flops | bytes accessed | tf_op | source)
XLA Modules:
  0.0 50.2 jit_solution(1901695179527439290)
XLA Ops:
  0.7 47.6 %shard_map.82 = bf16[32,64,128]{2,1,0:T(8,128)(2,1)} custom-call(s32[133]{0:T(256)} %parent.1, s32[5]{0:T(128)} %pages.1, s32[5]{0:T(128)} %owners.1, s32[1]{0:T(128)S(6)} %copy.10.leaf_len, bf16[32,64,128]{2,1,0:T(8,128)(2,1)} %queries.1, bf16[256,128]{1,0:T(8,128)(2,1)} %bitcast.4, bf16[80,128]{1,0:T(8,128)(2,1)} %bitcast.5, bf16[512,128]{1,0:T(8,128)(2,1)} %bitcast.3), custom_call_target="tpu_custom_call" | custom-call | tf_op jit(solution)/shard_map/pallas_call | solution.py:302
  48.3 1.9 %copy.11 = bf16[32,64,128]{2,1,0:T(8,128)(2,1)} copy(bf16[32,64,128]{2,1,0:T(8,128)(2,1)} %shard_map.82) | data formatting | bytes 1048576

commit v2 on v0

v2 whole, which is shorter than its diff:
```python
import jax
import jax.numpy as jnp
from jax import lax
from jax.experimental import pallas as pl
from jax.experimental.pallas import tpu as pltpu
from jax.sharding import PartitionSpec as P

MESH = pl.DeviceIdType.MESH
BF, F32, I32 = jnp.bfloat16, jnp.float32, jnp.int32
NEG = -1e30
ROWS_A, ROWS_B = 256,256

REL = (0, 1, -1, 3, -3, 4, -2, 2, -4, 6, -6, 7, -5, 5, -7, 8)
STEP = (0, -1, 1)
GROUPS = ((0, 1, 3), (3, 2, 9), (9, 2, 16))


def dot_t(a, b):
    return lax.dot_general(a, b, (((1,), (1,)), ((), ())), preferred_element_type=F32)


def kernel(
    parent_in, pages_in, owners_in, leaf_len_in, queries, fresh_in, pooled_in, leaf_in, out,
    parent, pages, owners, leaf_len, fresh, pooled, leaf,
    q_all, k1, v1, k3, v3, b1, b3, wide, fresh_out,
    z_own, z_mid, z_far, ready, ready8, held, other, m_ref, acc, o_all,
    zs, zr, ys, yr, es, er, cs, cr, qs, qr, fs, fr, os, orr, local,
):
    pool, x = lax.axis_index("pool"), lax.axis_index("tp")
    z, y, c = pool // 8, (pool // 2) % 4, pool % 2

    def at(dz=0, dy=0, dc=0, dx=0):
        place = ((z + dz + 16) % 16) * 8 + ((y + dy) % 4) * 2 + (c + dc) % 2
        return (place, (x + dx) % 4)

    targets = [(t, j) for j in (2, 1, 3, 0) for t in (1, 2, 0) if t or j]
    peers = [at(dz=3), at(dz=-3)] + [at(dz=STEP[t], dy=j) for t, j in targets]
    peers += [at(dx=1), at(dx=2), at(dx=3), at(dc=1)]
    barrier = pltpu.get_barrier_semaphore()
    for peer in peers:
        pl.semaphore_signal(barrier, inc=1, device_id=peer, device_id_type=MESH)

    def fetch(k, src, dst):
        copy = pltpu.make_async_copy(src, dst, local.at[k])
        copy.start()
        return copy

    get_pooled = fetch(0, pooled_in, pooled)
    get_fresh = fetch(1, fresh_in, fresh)
    scalars = [
        fetch(2, parent_in, parent),
        fetch(3, pages_in, pages),
        fetch(4, owners_in, owners),
        fetch(5, leaf_len_in, leaf_len),
    ]
    get_leaf = fetch(6, leaf_in, leaf)
    rows_x = pl.ds(pl.multiple_of(x * 32, 32), 32)
    heads = pl.ds(pl.multiple_of(x * 16, 16), 16)
    get_q = fetch(7, queries.at[:, heads], q_all.at[rows_x])

    get_pooled.wait()
    wide[0:80] = pooled[...].astype(F32)
    for n in range(5):
        keys = wide[pl.ds(16 * n, 8, stride=2)]
        values = wide[pl.ds(16 * n + 1, 8, stride=2)]
        z_own[0, n] = jnp.concatenate([keys, values], 0).astype(BF)

    def mids_at(dz, dy):
        first = at(dz=dz, dy=dy)[0] - c
        return [parent[5 + first], parent[6 + first]]

    pl.semaphore_wait(barrier, len(peers))

    started = []

    def send(src, dst, s, r, peer):
        copy = pltpu.make_async_remote_copy(
            src_ref=src, dst_ref=dst, send_sem=s, recv_sem=r, device_id=peer, device_id_type=MESH
        )
        copy.start()
        started.append(copy)
        return copy

    def send_z(k, src, dst, dz):
        return send(src, dst, zs.at[k], zr.at[k], at(dz=dz))

    threes = [
        send_z(0, z_own.at[0], z_mid.at[0], -3),
        send_z(1, z_own.at[0], z_mid.at[1], 3),
    ]

    q_in = []
    for j in (2, 1, 3):
        head = pl.multiple_of(((x + j) % 4) * 16, 16)
        q_in.append(
            send(queries.at[:, pl.ds(head, 16)], q_all.at[rows_x], qs.at[j - 1], qr.at[j - 1], at(dx=j))
        )

    def spread(g, zone):
        lo, n, _ = GROUPS[g]
        sets = pl.ds((0, 1, 3)[g], n)
        copies = []
        for t, j in targets:
            ready[t, j, 0, sets] = zone[:, 0]
            for cc in range(2):
                ready[t, j, 1 + cc, sets] = zone[:, mid[t][j][cc]]
            copies.append(
                send(
                    ready.at[t, j, :, sets],
                    held.at[:, (4 - j) % 4, pl.ds(lo + n * t, n)],
                    ys.at[g, t, j],
                    yr.at[g, t, j],
                    at(dz=STEP[t], dy=j),
                )
            )
        held[0, 0, lo : lo + n] = zone[:, 0]
        for cc in range(2):
            held[1 + cc, 0, lo : lo + n] = zone[:, mid[0][0][cc]]
        return copies

    for copy in scalars:
        copy.wait()
    mid = [[mids_at(STEP[t], j) for j in range(4)] for t in range(3)]
    first_in = spread(0, z_own)

    get_fresh.wait()
    wide[128:384] = fresh[...].astype(F32)
    for h in range(4):
        for kv in range(2):
            fresh_out[h, kv] = wide[pl.ds(128 + 2 * h + kv, 32, stride=8)].astype(BF)
    for j in (2, 1, 3):
        for kv in range(2):
            q_in.append(
                send(
                    fresh_out.at[(x + j) % 4, kv],
                    (k1 if kv == 0 else v1).at[rows_x, pl.ds(0, 128)],
                    fs.at[j - 1, kv],
                    fr.at[j - 1, kv],
                    at(dx=j),
                )
            )
    k1[rows_x, :] = fresh_out[x, 0]
    v1[rows_x, 0:128] = fresh_out[x, 1]

    get_leaf.wait()
    for part in range(2):
        wide[0:256] = leaf[pl.ds(part * 256, 256)].astype(F32)
        k1[128 + part * 128 : 256 + part * 128] = wide[pl.ds(0, 128, stride=2)].astype(BF)
        v1[128 + part * 128 : 256 + part * 128, 0:128] = wide[pl.ds(1, 128, stride=2)].astype(BF)
    v1[:, 128:256] = jnp.ones((1536, 128), BF)
    v3[:, 128:256] = jnp.ones((896, 128), BF)

    my_mid = parent[5 + pool]

    def used_bias(ref, col0, lo, hi):
        count = hi - lo
        block = 4 * count * 8
        col = lax.broadcasted_iota(I32, (8, 4 * block), 1)
        part = sum((col >= block * k).astype(I32) for k in range(1, 4))
        rest = col - part * block
        dy = sum((rest >= count * 8 * k).astype(I32) for k in range(1, 4))
        slot = (rest - dy * (count * 8)) // 8
        rel = jnp.zeros_like(slot)
        for k in range(count):
            rel = jnp.where(slot == k, (z + REL[lo + k] + 16) % 16, rel)
        core = jnp.where(part < 2, c, 1 - c)
        place = rel * 8 + ((y + dy) & 3) * 2 + core
        in_root = part % 2 == 0
        first = jnp.where(in_root, owners[0], owners[my_mid])
        many = jnp.where(in_root, pages[0], pages[my_mid])
        ref[:, col0 : col0 + 4 * block] = jnp.where(((place - first) & 127) < many, 0.0, NEG)

    b1[:, 0:256] = jnp.where(lax.broadcasted_iota(I32, (8, 256), 1) < leaf_len[0] * 8, 0.0, NEG)
    used_bias(b1, 256, 0, 3)

    for copy in threes:
        copy.wait_recv()
    sixes = [send_z(2, z_mid.at[0], z_far.at[0], -3), send_z(3, z_mid.at[1], z_far.at[1], 3)]
    second_in = spread(1, z_mid)

    used_bias(b1, 640, 3, 9)
    used_bias(b3, 0, 9, 16)

    def swap(g):
        slots = pl.ds(GROUPS[g][0], GROUPS[g][2] - GROUPS[g][0])
        return [
            send(held.at[0, :, slots], other.at[0, :, slots], cs.at[g, 0], cr.at[g, 0], at(dc=1)),
            send(held.at[2 - c, :, slots], other.at[1, :, slots], cs.at[g, 1], cr.at[g, 1], at(dc=1)),
        ]

    def gather_keys(k_ref, v_ref, row0, g, halves=(0, 1)):
        count = GROUPS[g][2] - GROUPS[g][0]
        size = 4 * count * 8
        slots = pl.ds(GROUPS[g][0], count)
        parts = (held.at[0, :, slots], held.at[1 + c, :, slots], other.at[0, :, slots], other.at[1, :, slots])
        for half in halves:
            for n in (2 * half, 2 * half + 1):
                blocks = parts[n][...].astype(F32).reshape(4 * count, 16, 128)
                to = slice(row0 + n * size, row0 + (n + 1) * size)
                k_ref[to] = blocks[:, 0:8].reshape(size, 128).astype(BF)
                v_ref[to, 0:128] = blocks[:, 8:16].reshape(size, 128).astype(BF)

    for copy in first_in:
        copy.wait_recv()
    first_swap = swap(0)

    for copy in sixes:
        copy.wait_recv()
    third_in = spread(2, z_far)
    for j in (2, 1, 3, 0):
        eight = mids_at(4 * c - 2, j)
        ready8[j, 0] = z_far[c, 0]
        for cc in range(2):
            ready8[j, 1 + cc] = z_far[c, eight[cc]]
        third_in.append(
            send(
                ready8.at[j],
                held.at[:, (4 - j) % 4, 15],
                es.at[j],
                er.at[j],
                at(dz=4 * c - 2, dy=j),
            )
        )

    for copy in second_in:
        copy.wait_recv()
    second_swap = swap(1)
    for copy in first_swap:
        copy.wait_recv()
    gather_keys(k1, v1, 384, 0)
    gather_keys(k1, v1, 768, 1, (0,))

    scale = (128 ** -0.5) * 1.4426950408889634

    def chunk(part, size):
        rows = pl.ds(pl.multiple_of(part * size, size), size)
        tokens = pl.ds(pl.multiple_of(part * (size // 16), size // 16), size // 16)
        return rows, tokens, q_all[tokens].reshape(size, 128)

    def start(part):
        rows, _, q = chunk(part, ROWS_A)
        s_new = dot_t(q, k1[0:128])
        row = part * (ROWS_A // 16) + lax.broadcasted_iota(I32, (ROWS_A, 128), 0) // 16
        s_new = jnp.where(lax.broadcasted_iota(I32, (ROWS_A, 128), 1) <= row, s_new, NEG)
        s_old = dot_t(q, k1[128:1536]) + b1[0:1]
        m = jnp.maximum(jnp.max(s_new, 1, keepdims=True), jnp.max(s_old, 1, keepdims=True))
        p_new = jnp.exp2((s_new - m) * scale).astype(BF)
        p_old = jnp.exp2((s_old - m) * scale).astype(BF)
        acc[rows] = jnp.dot(p_new, v1[0:128], preferred_element_type=F32) + jnp.dot(
            p_old, v1[128:1536], preferred_element_type=F32
        )
        m_ref[rows] = m

    get_q.wait()
    for copy in q_in:
        copy.wait_recv()
    for copy in second_swap:
        copy.wait_recv()
    gather_keys(k1, v1, 768, 1, (1,))
    for part in range(2048 // ROWS_A):
        if part == (2048 // ROWS_A) * 3 // 4:
            for copy in third_in:
                copy.wait_recv()
            third_swap = swap(2)
        start(part)
    gather_keys(k3, v3, 0, 2, (0,))
    for copy in third_swap:
        copy.wait_recv()
    gather_keys(k3, v3, 0, 2, (1,))

    results = []
    pieces = 512 // ROWS_B
    for j in (2, 1, 3, 0):
        for piece in range(pieces):
            rows, tokens, q = chunk((x + j) % 4 * pieces + piece, ROWS_B)
            s = dot_t(q, k3[...]) + b3[0:1]
            old = m_ref[rows]
            m = jnp.maximum(old, jnp.max(s, 1, keepdims=True))
            p = jnp.exp2((s - m) * scale).astype(BF)
            total = acc[rows] * jnp.exp2((old - m) * scale) + jnp.dot(
                p, v3[...], preferred_element_type=F32
            )
            tile = (total[:, 0:128] / total[:, 128:256]).astype(BF)
            o_all[tokens] = tile.reshape(ROWS_B // 16, 16, 128)
            there = out.at[pl.ds(piece * (ROWS_B // 16), ROWS_B // 16), heads]
            if j:
                results.append(
                    send(o_all.at[tokens], there, os.at[j - 1, piece], orr.at[j - 1, piece], at(dx=j))
                )
            else:
                results.append(fetch(8 + piece, o_all.at[tokens], there))
    for copy in started:
        copy.wait_send()
    for copy in results[: 3 * pieces]:
        copy.wait_recv()
    for copy in results[3 * pieces :]:
        copy.wait()


def per_device(queries, fresh, pooled, leaf, parent, pages, owners, leaf_len):
    dma = pltpu.SemaphoreType.DMA

    def zone(n):
        return pltpu.VMEM((n, 5, 16, 128), BF)

    return pl.pallas_call(
        kernel,
        out_shape=pltpu.VMEM((32, 64, 128), BF),
        in_specs=[pl.BlockSpec(memory_space=pltpu.HBM)] * 8,
        out_specs=pl.BlockSpec(memory_space=pltpu.VMEM),
        scratch_shapes=[
            pltpu.SMEM((133,), I32),
            pltpu.SMEM((5,), I32),
            pltpu.SMEM((5,), I32),
            pltpu.SMEM((1,), I32),
            pltpu.VMEM((256, 128), BF),
            pltpu.VMEM((80, 128), BF),
            pltpu.VMEM((512, 128), BF),
            pltpu.VMEM((128, 16, 128), BF),
            pltpu.VMEM((1536, 128), BF),
            pltpu.VMEM((1536, 256), BF),
            pltpu.VMEM((896, 128), BF),
            pltpu.VMEM((896, 256), BF),
            pltpu.VMEM((8, 1408), F32),
            pltpu.VMEM((8, 896), F32),
            pltpu.VMEM((384, 128), F32),
            pltpu.VMEM((4, 2, 32, 128), BF),
            zone(1),
            zone(2),
            zone(2),
            pltpu.VMEM((3, 4, 3, 5, 16, 128), BF),
            pltpu.VMEM((4, 3, 16, 128), BF),
            pltpu.VMEM((3, 4, 16, 16, 128), BF),
            pltpu.VMEM((2, 4, 16, 16, 128), BF),
            pltpu.VMEM((2048, 1), F32),
            pltpu.VMEM((2048, 256), F32),
            pltpu.VMEM((128, 16, 128), BF),
            dma((4,)),
            dma((4,)),
            dma((3, 3, 4)),
            dma((3, 3, 4)),
            dma((4,)),
            dma((4,)),
            dma((3, 2)),
            dma((3, 2)),
            dma((3,)),
            dma((3,)),
            dma((3, 2)),
            dma((3, 2)),
            dma((3, 512 // ROWS_B)),
            dma((3, 512 // ROWS_B)),
            dma((8 + 512 // ROWS_B,)),
        ],
        compiler_params=pltpu.CompilerParams(
            collective_id=0, has_side_effects=True, vmem_limit_bytes=56 << 20
        ),
    )(
        parent,
        pages,
        owners,
        leaf_len,
        queries,
        fresh.reshape(256, 128),
        pooled.reshape(80, 128),
        leaf.reshape(512, 128),
    )


def solution(mesh):
    return jax.shard_map(
        per_device,
        mesh=mesh,
        in_specs=(
            P(("pool", "tp"), None, None),
            P(("pool", "tp"), None, None, None),
            P(None, "pool", None, "tp", None, None),
            P("pool", None, "tp", None, None),
            P(),
            P(),
            P(),
            P("pool"),
        ),
        out_specs=P(("pool", "tp"), None, None),
        check_vma=False,
    )
```

time: 225 us -> 44.2 us (0.20)
  waiting for transfers between devices: 113 us -> 0 us
  Pallas kernels: 0 us -> 42.6 us
  matrix products: 35.1 us -> 0 us
  other arithmetic: 22.4 us -> 0 us
  between operations: 17.2 us -> 0.66 us
  local copies, waits for them, and re-layouts: 14.9 us -> 0.8 us
  blocking collectives: 12.8 us -> 0 us
  starting transfers between devices: 9.09 us -> 0 us
    all_gather x1 -> x0, waiting for transfers between devices: 109 us -> none  [per_device(): pieces = lax.all_gather(pooled_page_cache, 'pool', axis=1, tiled=True)]
    pallas_call x0 -> x1, Pallas kernels: none -> 42.6 us  [per_device(): pl.pallas_call(kernel, out_shape=pltpu.VMEM((32, 64, 128), BF), in_specs=...]
    dot_general x14 -> x0, matrix products: 35.1 us -> none  [the longest x7 21.2 us: attend(): jnp.einsum(value_form, weights.astype(jnp.bfloat16), key_pairs[..., 1, :]...]
    reduce_sum x7 -> x0, other arithmetic: 16 us -> none  [attend(): totals = totals * rescale + jnp.sum(weights, axis=-1)]
    all_to_all x1 -> x0, blocking collectives: 12.8 us -> none  [per_device(): return lax.all_to_all(result, 'tp', split_axis=0, concat_axis=1, tiled=True)]
    all_to_all x2 -> x0, starting transfers between devices: 9.09 us -> none  [the longest x1 4.84 us: per_device(): lax.all_to_all(fresh_key_values, 'tp', split_axis=1, concat_axis=0, tiled...]
    slice x5 -> x0, local copies, waits for them, and re-layouts: 7.39 us -> none  [the longest x2 3.18 us: per_device(): pieces[node_id].reshape(stripes * page_len, kv_local, 2, head_dim)]
    and x4 -> x0, other arithmetic: 5.03 us -> none  [per_device(): key_mask = relevant[:, None, None] & usable[None, None, :]]
  transfers between devices with their start and end apart: 3 -> 0, of which waited for: 2 -> 0; matrix products, arithmetic and copies ran while one was open for 8% -> 0% of each run, Pallas kernels for 0% -> 0%
where the time goes in v2:
time: 44.2 us; the launch traced here: 44.1 us
  Pallas kernels  42.6 us (96%)
  local copies, waits for them, and re-layouts  0.8 us (2%)
  between operations  0.66 us (1%)
    pallas_call x1, Pallas kernels, per_device(): pl.pallas_call(kernel, out_shape=pltpu.VMEM((32, 64, 128), BF), in_specs=...  42.6 us

profile of v2, /device:TPU:1, one launch (start us, length us, event | category | flops | bytes accessed | tf_op | source)
XLA Modules:
  0.0 44.1 jit_solution(18021584929885384905)
XLA Ops:
  0.7 42.6 %shard_map.82 = bf16[32,64,128]{2,1,0:T(8,128)(2,1)S(1)} custom-call(s32[133]{0:T(256)} %parent_in.1, s32[5]{0:T(128)} %pages_in.1, s32[5]{0:T(128)} %owners_in.1, s32[1]{0:T(128)S(6)} %copy.11.leaf_len_in, bf16[32,64,128]{2,1,0:T(8,128)(2,1)} %queries.1, bf16[256,128]{1,0:T(8,128)(2,1)} %bitcast.4, bf16[80,128]{1,0:T(8,128)(2,1)} %bitcast.5, ...), custom_call_target="tpu_custom_call" | custom-call | tf_op jit(solution)/shard_map/pallas_call | solution.py:306
  43.3 0.8 %copy.10 = bf16[32,64,128]{2,1,0:T(8,128)(2,1)} copy(bf16[32,64,128]{2,1,0:T(8,128)(2,1)S(1)} %shard_map.82) | data formatting | bytes 1048576

commit v3 on v2

--- a/solution.py
+++ b/solution.py
@@ -8,7 +8,8 @@
 MESH = pl.DeviceIdType.MESH
 BF, F32, I32 = jnp.bfloat16, jnp.float32, jnp.int32
 NEG = -1e30
-ROWS_A, ROWS_B = 256,256
+ROWS_A, ROWS_B = 256, 256
+WAIT_AT, AHEAD = 2, 2
 
 REL = (0, 1, -1, 3, -3, 4, -2, 2, -4, 6, -6, 7, -5, 5, -7, 8)
 STEP = (0, -1, 1)
@@ -22,7 +23,7 @@
 def kernel(
     parent_in, pages_in, owners_in, leaf_len_in, queries, fresh_in, pooled_in, leaf_in, out,
     parent, pages, owners, leaf_len, fresh, pooled, leaf,
-    q_all, k1, v1, k3, v3, b1, b3, wide, fresh_out,
+    q_all, k1, v1, k2, v2, k3, v3, b1, b2, b3, wide, fresh_out,
     z_own, z_mid, z_far, ready, ready8, held, other, m_ref, acc, o_all,
     zs, zr, ys, yr, es, er, cs, cr, qs, qr, fs, fr, os, orr, local,
 ):
@@ -34,7 +35,8 @@
         return (place, (x + dx) % 4)
 
     targets = [(t, j) for j in (2, 1, 3, 0) for t in (1, 2, 0) if t or j]
-    peers = [at(dz=3), at(dz=-3)] + [at(dz=STEP[t], dy=j) for t, j in targets]
+    peers = [at(dz=3), at(dz=-3)]
+    peers += [at(dz=STEP[t], dy=j) for t, j in targets]
     peers += [at(dx=1), at(dx=2), at(dx=3), at(dc=1)]
     barrier = pltpu.get_barrier_semaphore()
     for peer in peers:
@@ -66,8 +68,7 @@
         z_own[0, n] = jnp.concatenate([keys, values], 0).astype(BF)
 
     def mids_at(dz, dy):
-        first = at(dz=dz, dy=dy)[0] - c
-        return [parent[5 + first], parent[6 + first]]
+        return [parent[5 + at(dz=dz, dy=dy, dc=k)[0]] for k in (0, 1)]
 
     pl.semaphore_wait(barrier, len(peers))
 
@@ -99,23 +100,21 @@
     def spread(g, zone):
         lo, n, _ = GROUPS[g]
         sets = pl.ds((0, 1, 3)[g], n)
-        copies = []
+        copies = {}
         for t, j in targets:
-            ready[t, j, 0, sets] = zone[:, 0]
-            for cc in range(2):
-                ready[t, j, 1 + cc, sets] = zone[:, mid[t][j][cc]]
-            copies.append(
-                send(
-                    ready.at[t, j, :, sets],
-                    held.at[:, (4 - j) % 4, pl.ds(lo + n * t, n)],
-                    ys.at[g, t, j],
-                    yr.at[g, t, j],
-                    at(dz=STEP[t], dy=j),
-                )
+            ready[t, j, 0, sets] = zone[:, mid[t][j][0]]
+            ready[t, j, 1, sets] = zone[:, 0]
+            ready[t, j, 2, sets] = zone[:, mid[t][j][1]]
+            copies[t, j] = send(
+                ready.at[t, j, :, sets],
+                held.at[:, (4 - j) % 4, pl.ds(lo + n * t, n)],
+                ys.at[g, t, j],
+                yr.at[g, t, j],
+                at(dz=STEP[t], dy=j),
             )
-        held[0, 0, lo : lo + n] = zone[:, 0]
-        for cc in range(2):
-            held[1 + cc, 0, lo : lo + n] = zone[:, mid[0][0][cc]]
+        held[0, 0, lo : lo + n] = zone[:, mid[0][0][0]]
+        held[1, 0, lo : lo + n] = zone[:, 0]
+        held[2, 0, lo : lo + n] = zone[:, mid[0][0][1]]
         return copies
 
     for copy in scalars:
@@ -147,7 +146,8 @@
         wide[0:256] = leaf[pl.ds(part * 256, 256)].astype(F32)
         k1[128 + part * 128 : 256 + part * 128] = wide[pl.ds(0, 128, stride=2)].astype(BF)
         v1[128 + part * 128 : 256 + part * 128, 0:128] = wide[pl.ds(1, 128, stride=2)].astype(BF)
-    v1[:, 128:256] = jnp.ones((1536, 128), BF)
+    v1[:, 128:256] = jnp.ones((768, 128), BF)
+    v2[:, 128:256] = jnp.ones((768, 128), BF)
     v3[:, 128:256] = jnp.ones((896, 128), BF)
 
     my_mid = parent[5 + pool]
@@ -178,57 +178,42 @@
     sixes = [send_z(2, z_mid.at[0], z_far.at[0], -3), send_z(3, z_mid.at[1], z_far.at[1], 3)]
     second_in = spread(1, z_mid)
 
-    used_bias(b1, 640, 3, 9)
+    used_bias(b2, 0, 3, 9)
     used_bias(b3, 0, 9, 16)
 
-    def swap(g):
+    def swap(g, k, dys):
         slots = pl.ds(GROUPS[g][0], GROUPS[g][2] - GROUPS[g][0])
-        return [
-            send(held.at[0, :, slots], other.at[0, :, slots], cs.at[g, 0], cr.at[g, 0], at(dc=1)),
-            send(held.at[2 - c, :, slots], other.at[1, :, slots], cs.at[g, 1], cr.at[g, 1], at(dc=1)),
-        ]
-
-    def gather_keys(k_ref, v_ref, row0, g, halves=(0, 1)):
+        return send(held.at[1:3, dys, slots], other.at[:, dys, slots], cs.at[g, k], cr.at[g, k], at(dc=1))
+
+    def gather_keys(k_ref, v_ref, row0, g, which=(0, 1, 2, 3)):
         count = GROUPS[g][2] - GROUPS[g][0]
         size = 4 * count * 8
         slots = pl.ds(GROUPS[g][0], count)
-        parts = (held.at[0, :, slots], held.at[1 + c, :, slots], other.at[0, :, slots], other.at[1, :, slots])
-        for half in halves:
-            for n in (2 * half, 2 * half + 1):
-                blocks = parts[n][...].astype(F32).reshape(4 * count, 16, 128)
-                to = slice(row0 + n * size, row0 + (n + 1) * size)
-                k_ref[to] = blocks[:, 0:8].reshape(size, 128).astype(BF)
-                v_ref[to, 0:128] = blocks[:, 8:16].reshape(size, 128).astype(BF)
-
-    for copy in first_in:
-        copy.wait_recv()
-    first_swap = swap(0)
+        for n in which:
+            blocks = (held[1 - n, :, slots] if n < 2 else other[n - 2, :, slots]).astype(F32)
+            blocks = blocks.reshape(4 * count, 16, 128)
+            to = slice(row0 + n * size, row0 + (n + 1) * size)
+            k_ref[to] = blocks[:, 0:8].reshape(size, 128).astype(BF)
+            v_ref[to, 0:128] = blocks[:, 8:16].reshape(size, 128).astype(BF)
+
+    for copy in first_in.values():
+        copy.wait_recv()
+    first_swap = swap(0, 0, slice(0, 4))
 
     for copy in sixes:
         copy.wait_recv()
     third_in = spread(2, z_far)
+    eight_in = {}
     for j in (2, 1, 3, 0):
         eight = mids_at(4 * c - 2, j)
-        ready8[j, 0] = z_far[c, 0]
-        for cc in range(2):
-            ready8[j, 1 + cc] = z_far[c, eight[cc]]
-        third_in.append(
-            send(
-                ready8.at[j],
-                held.at[:, (4 - j) % 4, 15],
-                es.at[j],
-                er.at[j],
-                at(dz=4 * c - 2, dy=j),
-            )
+        ready8[j, 0] = z_far[c, eight[0]]
+        ready8[j, 1] = z_far[c, 0]
+        ready8[j, 2] = z_far[c, eight[1]]
+        eight_in[j] = send(
+            ready8.at[j], held.at[:, (4 - j) % 4, 15], es.at[j], er.at[j], at(dz=4 * c - 2, dy=j)
         )
-
-    for copy in second_in:
-        copy.wait_recv()
-    second_swap = swap(1)
-    for copy in first_swap:
-        copy.wait_recv()
+    first_swap.wait_recv()
     gather_keys(k1, v1, 384, 0)
-    gather_keys(k1, v1, 768, 1, (0,))
 
     scale = (128 ** -0.5) * 1.4426950408889634
 
@@ -242,53 +227,88 @@
         s_new = dot_t(q, k1[0:128])
         row = part * (ROWS_A // 16) + lax.broadcasted_iota(I32, (ROWS_A, 128), 0) // 16
         s_new = jnp.where(lax.broadcasted_iota(I32, (ROWS_A, 128), 1) <= row, s_new, NEG)
-        s_old = dot_t(q, k1[128:1536]) + b1[0:1]
+        s_old = dot_t(q, k1[128:768]) + b1[0:1]
         m = jnp.maximum(jnp.max(s_new, 1, keepdims=True), jnp.max(s_old, 1, keepdims=True))
         p_new = jnp.exp2((s_new - m) * scale).astype(BF)
         p_old = jnp.exp2((s_old - m) * scale).astype(BF)
         acc[rows] = jnp.dot(p_new, v1[0:128], preferred_element_type=F32) + jnp.dot(
-            p_old, v1[128:1536], preferred_element_type=F32
+            p_old, v1[128:768], preferred_element_type=F32
         )
         m_ref[rows] = m
 
+    def more(part):
+        rows, _, q = chunk(part, ROWS_A)
+        s = dot_t(q, k2[...]) + b2[0:1]
+        old = m_ref[rows]
+        m = jnp.maximum(old, jnp.max(s, 1, keepdims=True))
+        p = jnp.exp2((s - m) * scale).astype(BF)
+        acc[rows] = acc[rows] * jnp.exp2((old - m) * scale) + jnp.dot(
+            p, v2[...], preferred_element_type=F32
+        )
+        m_ref[rows] = m
+
     get_q.wait()
     for copy in q_in:
         copy.wait_recv()
-    for copy in second_swap:
-        copy.wait_recv()
-    gather_keys(k1, v1, 768, 1, (1,))
-    for part in range(2048 // ROWS_A):
-        if part == (2048 // ROWS_A) * 3 // 4:
-            for copy in third_in:
+    count = 2048 // ROWS_A
+    for part in range(count):
+        if part == count // 4:
+            for copy in second_in.values():
                 copy.wait_recv()
-            third_swap = swap(2)
+            second_swap = swap(1, 0, slice(0, 4))
         start(part)
-    gather_keys(k3, v3, 0, 2, (0,))
+    gather_keys(k2, v2, 0, 1, (0, 1))
+    second_swap.wait_recv()
+    gather_keys(k2, v2, 0, 1, (2, 3))
+    for part in range(count):
+        if part == WAIT_AT:
+            third_swap = []
+            for j in (0, 1, 3, 2):
+                for t in (0, 1, 2):
+                    if t or j:
+                        third_in[t, j].wait_recv()
+                eight_in[j].wait_recv()
+                third_swap.append(swap(2, j, (4 - j) % 4))
+        more(part)
+    gather_keys(k3, v3, 0, 2, (0, 1))
+
+    pieces = 512 // ROWS_B
+    order = [(j, piece) for j in (2, 1, 3, 0) for piece in range(pieces)]
+
+    def scores(j, piece, span):
+        _, _, q = chunk((x + j) % 4 * pieces + piece, ROWS_B)
+        return dot_t(q, k3[span]) + b3[0:1, span]
+
+    ahead = [scores(*step, slice(0, 448)) for step in order[:AHEAD]]
     for copy in third_swap:
         copy.wait_recv()
-    gather_keys(k3, v3, 0, 2, (1,))
+    gather_keys(k3, v3, 0, 2, (2, 3))
 
     results = []
-    pieces = 512 // ROWS_B
-    for j in (2, 1, 3, 0):
-        for piece in range(pieces):
-            rows, tokens, q = chunk((x + j) % 4 * pieces + piece, ROWS_B)
-            s = dot_t(q, k3[...]) + b3[0:1]
-            old = m_ref[rows]
-            m = jnp.maximum(old, jnp.max(s, 1, keepdims=True))
+    for number, (j, piece) in enumerate(order):
+        rows, tokens, _ = chunk((x + j) % 4 * pieces + piece, ROWS_B)
+        old = m_ref[rows]
+        if number < AHEAD:
+            parts = [ahead[number], scores(j, piece, slice(448, 896))]
+            spans = [slice(0, 448), slice(448, 896)]
+        else:
+            parts, spans = [scores(j, piece, slice(0, 896))], [slice(0, 896)]
+        m = old
+        for s in parts:
+            m = jnp.maximum(m, jnp.max(s, 1, keepdims=True))
+        total = acc[rows] * jnp.exp2((old - m) * scale)
+        for s, span in zip(parts, spans):
             p = jnp.exp2((s - m) * scale).astype(BF)
-            total = acc[rows] * jnp.exp2((old - m) * scale) + jnp.dot(
-                p, v3[...], preferred_element_type=F32
+            total += jnp.dot(p, v3[span], preferred_element_type=F32)
+        tile = (total[:, 0:128] / total[:, 128:256]).astype(BF)
+        o_all[tokens] = tile.reshape(ROWS_B // 16, 16, 128)
+        there = out.at[pl.ds(piece * (ROWS_B // 16), ROWS_B // 16), heads]
+        if j:
+            results.append(
+                send(o_all.at[tokens], there, os.at[j - 1, piece], orr.at[j - 1, piece], at(dx=j))
             )
-            tile = (total[:, 0:128] / total[:, 128:256]).astype(BF)
-            o_all[tokens] = tile.reshape(ROWS_B // 16, 16, 128)
-            there = out.at[pl.ds(piece * (ROWS_B // 16), ROWS_B // 16), heads]
-            if j:
-                results.append(
-                    send(o_all.at[tokens], there, os.at[j - 1, piece], orr.at[j - 1, piece], at(dx=j))
-                )
-            else:
-                results.append(fetch(8 + piece, o_all.at[tokens], there))
+        else:
+            results.append(fetch(8 + piece, o_all.at[tokens], there))
     for copy in started:
         copy.wait_send()
     for copy in results[: 3 * pieces]:
@@ -317,11 +337,14 @@
             pltpu.VMEM((80, 128), BF),
             pltpu.VMEM((512, 128), BF),
             pltpu.VMEM((128, 16, 128), BF),
-            pltpu.VMEM((1536, 128), BF),
-            pltpu.VMEM((1536, 256), BF),
+            pltpu.VMEM((768, 128), BF),
+            pltpu.VMEM((768, 256), BF),
+            pltpu.VMEM((768, 128), BF),
+            pltpu.VMEM((768, 256), BF),
             pltpu.VMEM((896, 128), BF),
             pltpu.VMEM((896, 256), BF),
-            pltpu.VMEM((8, 1408), F32),
+            pltpu.VMEM((8, 640), F32),
+            pltpu.VMEM((8, 768), F32),
             pltpu.VMEM((8, 896), F32),
             pltpu.VMEM((384, 128), F32),
             pltpu.VMEM((4, 2, 32, 128), BF),
@@ -341,8 +364,8 @@
             dma((3, 3, 4)),
             dma((4,)),
             dma((4,)),
-            dma((3, 2)),
-            dma((3, 2)),
+            dma((3, 4)),
+            dma((3, 4)),
             dma((3,)),
             dma((3,)),
             dma((3, 2)),

time: 44.2 us -> 42.2 us (0.955)
  Pallas kernels: 42.6 us -> 40.6 us
    pallas_call x1, Pallas kernels: 42.6 us -> 40.6 us  [per_device(): pl.pallas_call(kernel, out_shape=pltpu.VMEM((32, 64, 128), BF), in_specs=...]
where the time goes in v3:
time: 42.2 us; the launch traced here: 42.1 us
  Pallas kernels  40.6 us (96%)
  local copies, waits for them, and re-layouts  0.8 us (2%)
  between operations  0.66 us (2%)
    pallas_call x1, Pallas kernels, per_device(): pl.pallas_call(kernel, out_shape=pltpu.VMEM((32, 64, 128), BF), in_specs=...  40.6 us

profile of v3, /device:TPU:1, one launch (start us, length us, event | category | flops | bytes accessed | tf_op | source)
XLA Modules:
  0.0 42.1 jit_solution(1038007087974049200)
XLA Ops:
  0.7 40.6 %shard_map.82 = bf16[32,64,128]{2,1,0:T(8,128)(2,1)S(1)} custom-call(s32[133]{0:T(256)} %parent_in.1, s32[5]{0:T(128)} %pages_in.1, s32[5]{0:T(128)} %owners_in.1, s32[1]{0:T(128)S(6)} %copy.11.leaf_len_in, bf16[32,64,128]{2,1,0:T(8,128)(2,1)} %queries.1, bf16[256,128]{1,0:T(8,128)(2,1)} %bitcast.4, bf16[80,128]{1,0:T(8,128)(2,1)} %bitcast.5, ...), custom_call_target="tpu_custom_call" | custom-call | tf_op jit(solution)/shard_map/pallas_call | solution.py:326
  41.3 0.8 %copy.10 = bf16[32,64,128]{2,1,0:T(8,128)(2,1)} copy(bf16[32,64,128]{2,1,0:T(8,128)(2,1)S(1)} %shard_map.82) | data formatting | bytes 1048576

commit v4 on v3

--- a/solution.py
+++ b/solution.py
@@ -9,7 +9,7 @@
 BF, F32, I32 = jnp.bfloat16, jnp.float32, jnp.int32
 NEG = -1e30
 ROWS_A, ROWS_B = 256, 256
-WAIT_AT, AHEAD = 2, 2
+WAIT_AT, AHEAD = 1, 3
 
 REL = (0, 1, -1, 3, -3, 4, -2, 2, -4, 6, -6, 7, -5, 5, -7, 8)
 STEP = (0, -1, 1)
@@ -141,6 +141,11 @@
     k1[rows_x, :] = fresh_out[x, 0]
     v1[rows_x, 0:128] = fresh_out[x, 1]
 
+    for copy in threes:
+        copy.wait_recv()
+    sixes = [send_z(2, z_mid.at[0], z_far.at[0], -3), send_z(3, z_mid.at[1], z_far.at[1], 3)]
+    second_in = spread(1, z_mid)
+
     get_leaf.wait()
     for part in range(2):
         wide[0:256] = leaf[pl.ds(part * 256, 256)].astype(F32)
@@ -172,11 +177,6 @@
 
     b1[:, 0:256] = jnp.where(lax.broadcasted_iota(I32, (8, 256), 1) < leaf_len[0] * 8, 0.0, NEG)
     used_bias(b1, 256, 0, 3)
-
-    for copy in threes:
-        copy.wait_recv()
-    sixes = [send_z(2, z_mid.at[0], z_far.at[0], -3), send_z(3, z_mid.at[1], z_far.at[1], 3)]
-    second_in = spread(1, z_mid)
 
     used_bias(b2, 0, 3, 9)
     used_bias(b3, 0, 9, 16)

time: 42.2 us -> 41.8 us (level)
  no operation moved by 1% of the time
where the time goes in v4:
time: 41.8 us; the launch traced here: 41.7 us
  Pallas kernels  40.2 us (96%)
  local copies, waits for them, and re-layouts  0.8 us (2%)
  between operations  0.66 us (2%)
    pallas_call x1, Pallas kernels, per_device(): pl.pallas_call(kernel, out_shape=pltpu.VMEM((32, 64, 128), BF), in_specs=...  40.2 us

profile of v4, /device:TPU:1, one launch (start us, length us, event | category | flops | bytes accessed | tf_op | source)
XLA Modules:
  0.0 41.7 jit_solution(18415863218604004137)
XLA Ops:
  0.7 40.2 %shard_map.82 = bf16[32,64,128]{2,1,0:T(8,128)(2,1)S(1)} custom-call(s32[133]{0:T(256)} %parent_in.1, s32[5]{0:T(128)} %pages_in.1, s32[5]{0:T(128)} %owners_in.1, s32[1]{0:T(128)S(6)} %copy.11.leaf_len_in, bf16[32,64,128]{2,1,0:T(8,128)(2,1)} %queries.1, bf16[256,128]{1,0:T(8,128)(2,1)} %bitcast.4, bf16[80,128]{1,0:T(8,128)(2,1)} %bitcast.5, ...), custom_call_target="tpu_custom_call" | custom-call | tf_op jit(solution)/shard_map/pallas_call | solution.py:326
  40.9 0.8 %copy.10 = bf16[32,64,128]{2,1,0:T(8,128)(2,1)} copy(bf16[32,64,128]{2,1,0:T(8,128)(2,1)S(1)} %shard_map.82) | data formatting | bytes 1048576
